TPU v7x, 128 devices: a whole 4x4x4 slice. The times are simulated.
128 devices in a mesh: seq: 16 (over z, y_hi, core), blk: 8 (over y_lo, x).
Axes of the slice: x: 4, y: 4 (y_hi: 2, y_lo: 2; y = y_hi * 2 + y_lo), z: 4, core: 2. Of those that a mesh axis runs over, the one named last changes fastest.
Arguments:
- tokens: bfloat16 [16384, 8192], P('seq', 'blk'), may hold values from -6 to 6
- right_factor: bfloat16 [64, 128, 128], P('blk', 'seq'), may hold values from -0.5 to 0.5
- left_factor: bfloat16 [128, 64, 64], P('blk', 'seq'), may hold values from -0.75 to 0.75
- target: bfloat16 [16384, 8192], P('seq', 'blk'), may hold values from -4 to 4
Outputs:
- student: bfloat16 [16384, 8192], P('seq', 'blk')
- right_grad: float32 [64, 128, 128], P('blk', 'seq')
- left_grad: float32 [128, 64, 64], P('blk', 'seq')
All inputs are finite; a program needn't handle non-finite values.
Results may differ from a plain program's by a relative error of at most 0.017.
Values may be sent and summed in bfloat16 or wider, within the bound.
No kernel may reach another device: no remote copies, remote signals or barrier semaphores. Data moves between devices by JAX's collectives and lax.ppermute only.
A program may use at most 64 MiB of HBM per device.

v0:
```python
import jax
import jax.numpy as jnp
from jax import lax
from jax.sharding import PartitionSpec as P


def gelu_tanh(values):
    return jax.nn.gelu(values, approximate=True)


def shards(tokens, right_factor, left_factor, target):
    rows = tokens.shape[0]
    count = rows * lax.axis_size("seq")
    scale = 1.0 / jnp.sqrt(jnp.float32(count))
    right_full, left_full = (
        lax.all_gather(right_factor, "seq", axis=1, tiled=True),
        lax.all_gather(left_factor, "seq", axis=1, tiled=True),
    )
    nblocks = left_full.shape[1]
    local_blocks = right_full.shape[0]
    width = right_full.shape[1]
    inputs = tokens.reshape(rows, local_blocks, width)
    mixed = jnp.einsum(
        "tki,kci->tkc", inputs, right_full, preferred_element_type=jnp.float32
    ).astype(jnp.bfloat16)
    turned = lax.all_to_all(mixed, "blk", split_axis=2, concat_axis=1, tiled=True)
    turned, pre = (
        turned,
        jnp.einsum("tkc,cmk->tcm", turned, left_full, preferred_element_type=jnp.float32),
    )
    local_cols = pre.shape[1]
    act, back = jax.vjp(gelu_tanh, pre)
    student = act.reshape(rows, local_cols * nblocks).astype(jnp.bfloat16)
    residual = (act - target.reshape(rows, local_cols, nblocks).astype(jnp.float32)) * scale
    pre_grad = back(residual)[0].astype(jnp.bfloat16)
    turned_grad = jnp.einsum(
        "tcm,cmk->tkc", pre_grad, left_full, preferred_element_type=jnp.float32
    ).astype(jnp.bfloat16)
    mixed_grad = lax.all_to_all(turned_grad, "blk", split_axis=1, concat_axis=2, tiled=True)
    left_term = jnp.einsum("tcm,tkc->cmk", pre_grad, turned, preferred_element_type=jnp.float32)
    right_term = jnp.einsum("tkc,tki->kci", mixed_grad, inputs, preferred_element_type=jnp.float32)
    right_total, left_total = (
        lax.psum(right_term.astype(jnp.bfloat16), "seq").astype(jnp.float32),
        lax.psum(left_term.astype(jnp.bfloat16), "seq").astype(jnp.float32),
    )
    place = lax.axis_index("seq")
    right_rows = right_factor.shape[1]
    left_rows = left_factor.shape[1]
    right_grad = lax.dynamic_slice_in_dim(right_total, place * right_rows, right_rows, 1)
    left_grad = lax.dynamic_slice_in_dim(left_total, place * left_rows, left_rows, 1)
    return (student, right_grad, left_grad)


def solution(mesh):
    return jax.shard_map(
        shards,
        mesh=mesh,
        in_specs=(P("seq", "blk"), P("blk", "seq", None), P("blk", "seq", None), P("seq", "blk")),
        out_specs=(P("seq", "blk"), P("blk", "seq", None), P("blk", "seq", None)),
        check_vma=False,
    )
```

profile of v0, /device:TPU:1, one launch (start us, length us, event | category | flops | bytes accessed | tf_op | source)
XLA Modules:
  0.0 280.4 jit_solution(13000971417474091226)
XLA Ops:
  7.2 0.0 copy-start
  7.2 28.3 %all_gather.6 = bf16[8,128,128]{2,1,0:T(8,128)(2,1)S(1)} all-gather(bf16[8,8,128]{2,1,0:T(8,128)(2,1)} %param.5), channel_id=1, replica_groups=mesh['seq'=16,'blk'=8] {'seq'}, dimensions={1}, use_global_device_ids=true | all-gather | bytes 278528 | tf_op jit(solution)/shard_map/all_gather | solution.py:16
  35.5 0.7 convert_bitcast_fusion.1
  36.3 2.5 copy.14
  38.7 4.5 %all-to-all-start = ((bf16[1024,8,128]{0,1,2:T(8,128)(2,1)}), bf16[1024,8,128]{0,1,2:T(8,128)(2,1)}, u32[]{:S(2)}, u32[]{:S(2)}) async-start(bf16[1024,8,128]{0,1,2:T(8,128)(2,1)} %copy.14), calls=%async_computation | async-start | bytes 4194304 | tf_op jit(solution)/shard_map/all_to_all | solution.py:26
  43.2 0.0 copy-done.2
  43.2 4.1 %copy.18 = f32[1024,1024]{0,1:T(8,128)} copy(bf16[1024,1024]{1,0:T(8,128)(2,1)} %param.7) | data formatting | bytes 6291456 | tf_op jit(solution)/shard_map/convert_element_type | solution.py:34
  47.4 31.7 %all_gather.7 = bf16[16,64,64]{2,0,1:T(8,128)(2,1)S(1)} all-gather(bf16[16,4,64]{2,0,1:T(8,128)(2,1)S(1)} %copy.16), channel_id=1, replica_groups=mesh['seq'=16,'blk'=8] {'seq'}, dimensions={1}, use_global_device_ids=true | all-gather | bytes 139264 | tf_op jit(solution)/shard_map/all_gather | solution.py:17
  79.1 0.0 all-to-all-done
  79.1 7.1 %fusion.6 = (bf16[1024,16,64]{0,2,1:T(8,128)(2,1)S(1)}, bf16[1024,16,64]{0,2,1:T(8,128)(2,1)}) fusion(f32[1024,16,64]{0,2,1:T(8,128)} %bitcast.61, bf16[1024,8,8,16]{0,1,3,2:T(8,128)(2,1)} %bitcast.1, bf16[16,64,64]{2,0,1:T(8,128)(2,1)S(1)} %all_gather.7), kind=kOutput, calls=%fused_computation.8 | convolution fusion | flops 159383552 | bytes 10616832 | tf_op jit(solution)/shard_map/tkc,cmk->tcm/dot_general | solution.py:29
  86.2 0.8 convert_bitcast_fusion
  87.0 0.6 copy-done.1
  87.5 2.5 copy.20
  90.0 11.2 %all-to-all-start.1 = ((bf16[1024,64,16]{0,2,1:T(8,128)(2,1)}), bf16[1024,64,16]{0,2,1:T(8,128)(2,1)}, u32[]{:S(2)}, u32[]{:S(2)}) async-start(bf16[1024,64,16]{0,2,1:T(8,128)(2,1)} %copy.20), calls=%async_computation.1 | async-start | bytes 4194304 | tf_op jit(solution)/shard_map/all_to_all | solution.py:39
  101.2 0.0 all-reduce.3.cloned.1.call-start
  101.3 3.7 %fusion.24 = bf16[16,64,64]{2,1,0:T(8,128)(2,1)} fusion(bf16[1024,16,64]{0,2,1:T(8,128)(2,1)} %copy-done.1, bf16[1024,8,8,16]{0,1,3,2:T(8,128)(2,1)} %bitcast.1), kind=kOutput, calls=%fused_computation.28 | convolution fusion | flops 134283264 | bytes 4325376 | tf_op jit(solution)/shard_map/tcm,tkc->cmk/dot_general | solution.py:40
  104.9 23.5 %all-to-all-done.1 = bf16[1024,64,16]{0,2,1:T(8,128)(2,1)} async-done(((bf16[1024,64,16]{0,2,1:T(8,128)(2,1)}), bf16[1024,64,16]{0,2,1:T(8,128)(2,1)}, u32[]{:S(2)}, u32[]{:S(2)}) %all-to-all-start.1) | async-done | bytes 2097184 | tf_op jit(solution)/shard_map/all_to_all | solution.py:39
  128.4 1.8 copy.21
  130.2 1.5 fusion.27
  131.7 0.0 all-reduce.3.cloned.1.call-update
  131.8 3.9 %copy.23 = bf16[1024,1024]{1,0:T(8,128)(2,1)} copy(bf16[1024,1024]{0,1:T(8,128)(2,1)} %bitcast.62) | data formatting | bytes 4194304
  135.7 135.1 %all-reduce.3.cloned.1.call-done = (bf16[8,128,128]{2,1,0:T(8,128)(2,1)}, bf16[16,64,64]{2,1,0:T(8,128)(2,1)}) async-done(((bf16[8,128,128]{2,1,0:T(8,128)(2,1)}, bf16[16,64,64]{2,1,0:T(8,128)(2,1)}), (bf16[8,128,128]{2,1,0:T(8,128)(2,1)}, bf16[16,64,64]{2,1,0:T(8,128)(2,1)})) %all-reduce.3.cloned.1.call-update) | async-done | bytes 393232 | tf_op jit(solution)/shard_map/psum | solution.py:43
  270.8 1.4 dynamic-slice_convert_fusion
  272.2 1.3 dynamic-slice_convert_fusion.1
  (4 shorter events, 0.0 us)
Async XLA Ops:
  7.2 28.4 %copy-start = (bf16[1024,1024]{1,0:T(8,128)(2,1)S(1)}, bf16[1024,1024]{1,0:T(8,128)(2,1)}, u32[]{:S(2)}) copy-start(bf16[1024,1024]{1,0:T(8,128)(2,1)} %param.4) | copy-start | bytes 6291460
  38.7 4.5 %copy-start.2 = (bf16[16,4,64]{2,1,0:T(4,128)(2,1)S(1)}, bf16[16,4,64]{2,1,0:T(4,128)(2,1)}, u32[]{:S(2)}) copy-start(bf16[16,4,64]{2,1,0:T(4,128)(2,1)} %param.6) | copy-start | bytes 24580
  38.7 40.4 %all-to-all-start = ((bf16[1024,8,128]{0,1,2:T(8,128)(2,1)}), bf16[1024,8,128]{0,1,2:T(8,128)(2,1)}, u32[]{:S(2)}, u32[]{:S(2)}) async-start(bf16[1024,8,128]{0,1,2:T(8,128)(2,1)} %copy.14), calls=%async_computation | async-start | bytes 4194304 | tf_op jit(solution)/shard_map/all_to_all | solution.py:26
  86.2 1.3 copy-start.1
  90.0 38.4 %all-to-all-start.1 = ((bf16[1024,64,16]{0,2,1:T(8,128)(2,1)}), bf16[1024,64,16]{0,2,1:T(8,128)(2,1)}, u32[]{:S(2)}, u32[]{:S(2)}) async-start(bf16[1024,64,16]{0,2,1:T(8,128)(2,1)} %copy.20), calls=%async_computation.1 | async-start | bytes 4194304 | tf_op jit(solution)/shard_map/all_to_all | solution.py:39
  101.2 169.6 %all-reduce.3.cloned.1.call-start = ((), (), s32[]{:S(2)}) async-start(), calls=%async_computation.2 | async-start | bytes 1048576 | tf_op jit(solution)/shard_map/psum | solution.py:43
Sparse Core Ops, SparseCore 0:
  131.9 138.8 all-reduce.2
where the time goes:
time: 281 us; the launch traced here: 280 us
  waiting for transfers between devices  159 us (57%)
  blocking collectives  60.1 us (21%)
  starting transfers between devices  15.7 us (6%)
  local copies, waits for them, and re-layouts  15.4 us (5%)
  between operations  14.1 us (5%)
  matrix products  13.8 us (5%)
    psum x1, waiting for transfers between devices, shards(): lax.psum(right_term.astype(jnp.bfloat16), 'seq').astype(jnp.float32)  135 us
    all_gather x1, blocking collectives, shards(): lax.all_gather(left_factor, 'seq', axis=1, tiled=True)  31.7 us
    all_gather x1, blocking collectives, shards(): lax.all_gather(right_factor, 'seq', axis=1, tiled=True)  28.3 us
    all_to_all x1, waiting for transfers between devices, shards(): lax.all_to_all(turned_grad, 'blk', split_axis=1, concat_axis=2, tiled=True)  23.5 us
    all_to_all x1, starting transfers between devices, shards(): lax.all_to_all(turned_grad, 'blk', split_axis=1, concat_axis=2, tiled=True)  11.2 us
    dot_general x1, matrix products, shards(): jnp.einsum('tkc,cmk->tcm', turned, left_full, preferred_element_type=jnp....  7.07 us
  transfers between devices with their start and end apart: 3, of which 2 were waited for; matrix products, arithmetic and copies ran while one was open for 4% of the time, Pallas kernels for 0%

commit v1 on v0

--- a/solution.py
+++ b/solution.py
@@ -13,7 +13,9 @@
     count = rows * lax.axis_size("seq")
     scale = 1.0 / jnp.sqrt(jnp.float32(count))
     right_full, left_full = (
-        lax.all_gather(right_factor, "seq", axis=1, tiled=True),
+        jnp.concatenate(
+            lax.all_to_all(jnp.stack([right_factor] * lax.axis_size("seq")), "seq", 0, 0), axis=1
+        ),
         lax.all_gather(left_factor, "seq", axis=1, tiled=True),
     )
     nblocks = left_full.shape[1]

time: 281 us -> 271 us (0.964)
  blocking collectives: 60.1 us -> 52.4 us
    all_gather x1 -> x0, blocking collectives: 28.3 us -> none  [shards(): lax.all_gather(right_factor, 'seq', axis=1, tiled=True)]
    all_to_all x0 -> x1, blocking collectives: none -> 17.9 us  [shards(): lax.all_to_all(jnp.stack([right_factor] * lax.axis_size('seq')), 'seq', 0...]
    all_to_all x1, starting transfers between devices: 11.2 us -> 8.37 us  [shards(): lax.all_to_all(turned_grad, 'blk', split_axis=1, concat_axis=2, tiled=True)]
where the time goes in v1:
time: 271 us
  waiting for transfers between devices  158 us (58%)
  blocking collectives  52.4 us (19%)
  local copies, waits for them, and re-layouts  16.3 us (6%)
  between operations  14.1 us (5%)
  matrix products  13.8 us (5%)
  starting transfers between devices  12.9 us (5%)
  other arithmetic  2.71 us (1%)
    psum x1, waiting for transfers between devices, shards(): lax.psum(right_term.astype(jnp.bfloat16), 'seq').astype(jnp.float32)  135 us
    all_gather x1, blocking collectives, shards(): lax.all_gather(left_factor, 'seq', axis=1, tiled=True)  34.5 us
    all_to_all x1, waiting for transfers between devices, shards(): lax.all_to_all(turned_grad, 'blk', split_axis=1, concat_axis=2, tiled=True)  23.5 us
    all_to_all x1, blocking collectives, shards(): lax.all_to_all(jnp.stack([right_factor] * lax.axis_size('seq')), 'seq', 0...  17.9 us
    all_to_all x1, starting transfers between devices, shards(): lax.all_to_all(turned_grad, 'blk', split_axis=1, concat_axis=2, tiled=True)  8.37 us
    dot_general x1, matrix products, shards(): jnp.einsum('tkc,cmk->tcm', turned, left_full, preferred_element_type=jnp....  7.07 us
  transfers between devices with their start and end apart: 3, of which 2 were waited for; matrix products, arithmetic and copies ran while one was open for 4% of the time, Pallas kernels for 0%

profile of v1, /device:TPU:1, one launch (start us, length us, event | category | flops | bytes accessed | tf_op | source)
XLA Modules:
  0.0 270.7 jit_solution(14488494304396283827)
XLA Ops:
  7.2 0.0 copy-start
  7.2 0.9 stack.2
  8.1 17.9 %all_to_all.41 = bf16[16,8,8,128]{3,2,1,0:T(8,128)(2,1)S(1)} all-to-all(bf16[16,8,8,128]{3,2,1,0:T(8,128)(2,1)S(1)} %stack.2), channel_id=1, replica_groups=mesh['seq'=16,'blk'=8] {'seq'}, dimensions={0} | all-to-all | bytes 524288 | tf_op jit(solution)/shard_map/all_to_all | solution.py:17
  26.0 0.7 convert_bitcast_fusion.1
  26.8 2.5 copy.15
  29.2 4.5 %all-to-all-start.1 = ((bf16[1024,8,128]{0,1,2:T(8,128)(2,1)}), bf16[1024,8,128]{0,1,2:T(8,128)(2,1)}, u32[]{:S(2)}, u32[]{:S(2)}) async-start(bf16[1024,8,128]{0,1,2:T(8,128)(2,1)} %copy.15), calls=%async_computation.1 | async-start | bytes 4194304 | tf_op jit(solution)/shard_map/all_to_all | solution.py:28
  33.8 4.1 %copy.19 = f32[1024,1024]{0,1:T(8,128)} copy(bf16[1024,1024]{1,0:T(8,128)(2,1)} %param.7) | data formatting | bytes 6291456 | tf_op jit(solution)/shard_map/convert_element_type | solution.py:36
  37.9 34.5 %all_gather.3 = bf16[16,64,64]{2,0,1:T(8,128)(2,1)S(1)} all-gather(bf16[16,4,64]{2,0,1:T(8,128)(2,1)S(1)} %copy.17), channel_id=1, replica_groups=mesh['seq'=16,'blk'=8] {'seq'}, dimensions={1}, use_global_device_ids=true | all-gather | bytes 139264 | tf_op jit(solution)/shard_map/all_gather | solution.py:19
  72.4 0.0 all-to-all-done.1
  72.4 7.1 %fusion.6 = (bf16[1024,16,64]{0,2,1:T(8,128)(2,1)S(1)}, bf16[1024,16,64]{0,2,1:T(8,128)(2,1)}) fusion(f32[1024,16,64]{0,2,1:T(8,128)} %bitcast.67, bf16[1024,8,8,16]{0,1,3,2:T(8,128)(2,1)} %bitcast.3, bf16[16,64,64]{2,0,1:T(8,128)(2,1)S(1)} %all_gather.3), kind=kOutput, calls=%fused_computation.8 | convolution fusion | flops 159383552 | bytes 10616832 | tf_op jit(solution)/shard_map/tkc,cmk->tcm/dot_general | solution.py:31
  79.5 0.8 convert_bitcast_fusion
  80.2 0.6 copy-done.1
  80.8 2.5 copy.21
  83.3 8.4 %all-to-all-start.2 = ((bf16[1024,64,16]{0,2,1:T(8,128)(2,1)}), bf16[1024,64,16]{0,2,1:T(8,128)(2,1)}, u32[]{:S(2)}, u32[]{:S(2)}) async-start(bf16[1024,64,16]{0,2,1:T(8,128)(2,1)} %copy.21), calls=%async_computation.2 | async-start | bytes 4194304 | tf_op jit(solution)/shard_map/all_to_all | solution.py:41
  91.6 0.0 all-reduce.3.cloned.1.call-start
  91.7 3.7 %fusion.24 = bf16[16,64,64]{2,1,0:T(8,128)(2,1)} fusion(bf16[1024,16,64]{0,2,1:T(8,128)(2,1)} %copy-done.1, bf16[1024,8,8,16]{0,1,3,2:T(8,128)(2,1)} %bitcast.3), kind=kOutput, calls=%fused_computation.28 | convolution fusion | flops 134283264 | bytes 4325376 | tf_op jit(solution)/shard_map/tcm,tkc->cmk/dot_general | solution.py:42
  95.4 23.5 %all-to-all-done.2 = bf16[1024,64,16]{0,2,1:T(8,128)(2,1)} async-done(((bf16[1024,64,16]{0,2,1:T(8,128)(2,1)}), bf16[1024,64,16]{0,2,1:T(8,128)(2,1)}, u32[]{:S(2)}, u32[]{:S(2)}) %all-to-all-start.2) | async-done | bytes 2097184 | tf_op jit(solution)/shard_map/all_to_all | solution.py:41
  118.9 1.8 copy.22
  120.6 1.5 fusion.27
  122.2 0.0 all-reduce.3.cloned.1.call-update
  122.2 3.9 %copy.24 = bf16[1024,1024]{1,0:T(8,128)(2,1)} copy(bf16[1024,1024]{0,1:T(8,128)(2,1)} %bitcast.68) | data formatting | bytes 4194304
  126.1 135.0 %all-reduce.3.cloned.1.call-done = (bf16[8,128,128]{2,1,0:T(8,128)(2,1)}, bf16[16,64,64]{2,1,0:T(8,128)(2,1)}) async-done(((bf16[8,128,128]{2,1,0:T(8,128)(2,1)}, bf16[16,64,64]{2,1,0:T(8,128)(2,1)}), (bf16[8,128,128]{2,1,0:T(8,128)(2,1)}, bf16[16,64,64]{2,1,0:T(8,128)(2,1)})) %all-reduce.3.cloned.1.call-update) | async-done | bytes 393232 | tf_op jit(solution)/shard_map/psum | solution.py:45
  261.1 1.4 dynamic-slice_convert_fusion
  262.5 1.3 dynamic-slice_convert_fusion.1
  (5 shorter events, 0.0 us)
Async XLA Ops:
  7.2 18.9 %copy-start = (bf16[1024,1024]{1,0:T(8,128)(2,1)S(1)}, bf16[1024,1024]{1,0:T(8,128)(2,1)}, u32[]{:S(2)}) copy-start(bf16[1024,1024]{1,0:T(8,128)(2,1)} %param.4) | copy-start | bytes 6291460
  29.2 4.5 %copy-start.2 = (bf16[16,4,64]{2,1,0:T(4,128)(2,1)S(1)}, bf16[16,4,64]{2,1,0:T(4,128)(2,1)}, u32[]{:S(2)}) copy-start(bf16[16,4,64]{2,1,0:T(4,128)(2,1)} %param.6) | copy-start | bytes 24580
  29.2 43.2 %all-to-all-start.1 = ((bf16[1024,8,128]{0,1,2:T(8,128)(2,1)}), bf16[1024,8,128]{0,1,2:T(8,128)(2,1)}, u32[]{:S(2)}, u32[]{:S(2)}) async-start(bf16[1024,8,128]{0,1,2:T(8,128)(2,1)} %copy.15), calls=%async_computation.1 | async-start | bytes 4194304 | tf_op jit(solution)/shard_map/all_to_all | solution.py:28
  79.5 1.3 copy-start.1
  83.3 35.6 %all-to-all-start.2 = ((bf16[1024,64,16]{0,2,1:T(8,128)(2,1)}), bf16[1024,64,16]{0,2,1:T(8,128)(2,1)}, u32[]{:S(2)}, u32[]{:S(2)}) async-start(bf16[1024,64,16]{0,2,1:T(8,128)(2,1)} %copy.21), calls=%async_computation.2 | async-start | bytes 4194304 | tf_op jit(solution)/shard_map/all_to_all | solution.py:41
  91.6 169.5 %all-reduce.3.cloned.1.call-start = ((), (), s32[]{:S(2)}) async-start(), calls=%async_computation.3 | async-start | bytes 1048576 | tf_op jit(solution)/shard_map/psum | solution.py:45
Sparse Core Ops, SparseCore 0:
  122.3 138.7 all-reduce.2
